TPU v7x, 32 devices: a whole 2x2x4 slice. The times are simulated.
32 devices in a mesh: group: 2 (over y), dp: 8 (over z, x), shard: 2 (over core).
Axes of the slice: x: 2, y: 2, z: 4, core: 2. Of those that a mesh axis runs over, the one named last changes fastest.
Arguments:
- inputs: bfloat16 [32, 16, 32, 256], P(('group', 'dp', 'shard')), parts along dimension 0, may hold values from -6 to 6
- cotangent: bfloat16 [32, 16, 32, 256], P(('group', 'dp', 'shard')), parts along dimension 0, may hold values from -6 to 6
- conv_first: bfloat16 [18, 256, 256], P('group', None, 'shard'), parts along dimension 0, may hold values from -0.125 to 0.125
- conv_second: bfloat16 [18, 256, 256], P('group', None, 'shard'), parts along dimension 0, may hold values from -0.125 to 0.125
Outputs:
- outputs: bfloat16 [32, 16, 32, 256], P(('group', 'dp', 'shard')), parts along dimension 0
- grad_first: bfloat16 [18, 256, 256], P('group', None, 'shard'), parts along dimension 0
- grad_second: bfloat16 [18, 256, 256], P('group', None, 'shard'), parts along dimension 0
There are 2 independent parts, one for each index of `group`. A program takes and returns all parts, laid end to end along the dimension named above; each array names one. Nothing has to cross between parts.
All inputs are finite; a program needn't handle non-finite values.
Results may differ from a plain program's by a relative error of at most 0.012.
Values may be sent and summed in bfloat16 or wider, within the bound.
A program may use at most 64 MiB of HBM per device.

v0:
```python
import jax
import jax.numpy as jnp
from jax import lax
from jax.sharding import PartitionSpec as P


def conv_taps(field, kernel):
    samples, rows, cols, chans = field.shape
    padded = jnp.pad(field, ((0, 0), (1, 1), (1, 1), (0, 0)))
    total = jnp.zeros((samples * rows * cols, kernel.shape[2]), jnp.float32)
    for tap in range(9):
        above = tap // 3
        left = tap % 3
        window = padded[:, above : above + rows, left : left + cols, :].reshape(-1, chans)
        total = total + jnp.dot(window, kernel[tap], preferred_element_type=jnp.float32)
    return total.reshape(samples, rows, cols, kernel.shape[2])


def flipped(kernel):
    return jnp.transpose(kernel[::-1], (0, 2, 1))


def weight_terms(field, grad):
    samples, rows, cols, chans = field.shape
    padded = jnp.pad(field, ((0, 0), (1, 1), (1, 1), (0, 0)))
    grad_flat = grad.reshape(-1, grad.shape[3])
    terms = []
    for tap in range(9):
        above = tap // 3
        left = tap % 3
        window = padded[:, above : above + rows, left : left + cols, :].reshape(-1, chans)
        terms.append(
            lax.dot_general(
                window, grad_flat, (((0,), (0,)), ((), ())), preferred_element_type=jnp.float32
            )
        )
    return jnp.stack(terms, 0)


def body(inputs, cotangent, conv_first, conv_second):
    pre = conv_taps(inputs, lax.all_gather(conv_first, "shard", axis=2, tiled=True))
    hidden = jax.nn.silu(pre).astype(jnp.bfloat16)
    outputs = (
        inputs.astype(jnp.float32)
        + conv_taps(hidden, lax.all_gather(conv_second, "shard", axis=2, tiled=True))
    ).astype(jnp.bfloat16)
    back = conv_taps(cotangent, flipped(lax.all_gather(conv_second, "shard", axis=2, tiled=True)))
    sigma = jax.nn.sigmoid(pre)
    dpre = (back * sigma * (1.0 + pre * (1.0 - sigma))).astype(jnp.bfloat16)
    scale = 1.0 / (inputs.shape[0] * lax.axis_size("dp") * lax.axis_size("shard"))
    second_part = weight_terms(hidden, cotangent)
    first_part = weight_terms(inputs, dpre)
    first_half, second_half = (
        lax.psum_scatter(
            first_part.astype(jnp.bfloat16), "shard", scatter_dimension=2, tiled=True
        ).astype(jnp.float32),
        lax.psum_scatter(
            second_part.astype(jnp.bfloat16), "shard", scatter_dimension=2, tiled=True
        ).astype(jnp.float32),
    )
    first_sum, second_sum = lax.psum((first_half, second_half), "dp")
    grad_first = (first_sum * scale).astype(jnp.bfloat16)
    grad_second = (second_sum * scale).astype(jnp.bfloat16)
    return (outputs, grad_first, grad_second)


def solution(mesh):
    placed = (
        P(("group", "dp", "shard"), None, None, None),
        P(("group", "dp", "shard"), None, None, None),
        P("group", None, "shard"),
        P("group", None, "shard"),
    )
    return jax.shard_map(
        body,
        mesh=mesh,
        in_specs=placed,
        out_specs=(
            P(("group", "dp", "shard"), None, None, None),
            P("group", None, "shard"),
            P("group", None, "shard"),
        ),
        check_vma=False,
    )
```

profile of v0, /device:TPU:0, one launch (start us, length us, event | category | flops | bytes accessed | tf_op | source)
XLA Modules:
  0.0 177.9 jit_solution(16371178094781244886)
XLA Ops:
  8.0 0.7 all-gather.3.cloned.1.call-update
  8.7 1.1 pad_slice_fusion.16
  9.8 1.4 pad_slice_fusion
  11.2 10.2 %all-gather.5.cloned.1.call-done = bf16[9,256,256]{2,1,0:T(8,128)(2,1)} async-done(((bf16[9,256,128]{2,1,0:T(8,128)(2,1)}), bf16[9,256,256]{2,1,0:T(8,128)(2,1)}) %all-gather.5.cloned.1.call-update) | async-done | bytes 1179664 | tf_op jit(solution)/shard_map/all_gather | solution.py:45
  21.4 1.4 reverse_bitcast_fusion
  26.0 1.0 convolution_add_fusion.1
  27.1 6.3 %all-gather.3.cloned.1.call-done = bf16[9,256,256]{2,1,0:T(8,128)(2,1)} async-done(((bf16[9,256,128]{2,1,0:T(8,128)(2,1)}), bf16[9,256,256]{2,1,0:T(8,128)(2,1)}) %all-gather.3.cloned.1.call-update) | async-done | bytes 1179664 | tf_op jit(solution)/shard_map/all_gather | solution.py:41
  33.4 1.2 fusion.85
  34.6 1.1 convolution_add_fusion.23
  37.6 1.0 multiply_convert_fusion.2
  42.0 2.2 %copy.11 = bf16[9,256,256]{1,0,2:T(8,128)(2,1)S(1)} copy(bf16[9,256,256]{2,1,0:T(8,128)(2,1)S(1)} %fusion.40) | data formatting | bytes 2359296
  44.1 1.6 copy.15
  46.0 0.8 copy-done.15
  50.1 2.2 %copy.13 = bf16[9,256,256]{1,0,2:T(8,128)(2,1)S(1)} copy(bf16[9,256,256]{2,1,0:T(8,128)(2,1)S(1)} %fusion.22) | data formatting | bytes 2359296
  52.3 1.5 copy.16
  54.2 1.3 copy-done
  58.1 0.8 add_convert_fusion
  58.9 1.4 reshape.326
  60.3 0.8 copy.12
  61.2 6.6 %reduce-scatter.9.cloned.1.call-done = bf16[128,2304]{1,0:T(8,128)(2,1)} async-done(((bf16[256,2304]{1,0:T(8,128)(2,1)}), bf16[128,2304]{1,0:T(8,128)(2,1)}) %reduce-scatter.9.cloned.1.call-update) | async-done | bytes 589840
  67.8 1.4 reshape.328
  69.2 0.8 copy.14
  70.0 98.7 %all-reduce.5 = (f32[9,256,128]{2,1,0:T(8,128)S(1)}, f32[9,256,128]{2,1,0:T(8,128)}) all-reduce(bf16[9,256,128]{2,1,0:T(8,128)(2,1)S(1)} %copy.12, bf16[9,256,128]{2,1,0:T(8,128)(2,1)S(1)} %copy.14), channel_id=1, replica_groups=mesh['group'=2,'dp'=8,'shard'=2] {'dp'}, use_global_device_ids=true, to_apply=%region_1.2 | all-reduce | flops 589824 | bytes 3538944 | tf_op jit(solution)/shard_map/psum | solution.py:61
  168.8 2.5 %multiply_convert_fusion = (bf16[9,256,128]{2,1,0:T(8,128)(2,1)}, bf16[9,256,128]{2,1,0:T(8,128)(2,1)}) fusion(f32[9,256,128]{2,1,0:T(8,128)} %get-tuple-element.4, f32[9,256,128]{2,1,0:T(8,128)S(1)} %get-tuple-element.3), kind=kLoop, calls=%fused_computation.27 | loop fusion | flops 1179648 | bytes 3538944 | tf_op jit(solution)/shard_map/convert_element_type | solution.py:63
  (91 shorter events, 15.4 us)
Async XLA Ops:
  7.2 1.6 copy-start.1
  7.2 14.3 %all-gather.5.cloned.1.call-start = ((), (), s32[]{:S(2)}) async-start(), calls=%async_computation.3 | async-start | bytes 1769472 | tf_op jit(solution)/shard_map/all_gather | solution.py:45
  7.9 25.5 %all-gather.3.cloned.1.call-start = ((), (), s32[]{:S(2)}) async-start(), calls=%async_computation.2 | async-start | bytes 1769472 | tf_op jit(solution)/shard_map/all_gather | solution.py:41
  8.7 1.2 copy-start.4
  8.7 50.3 %reduce-scatter.7.cloned.1.call-start = ((), (), s32[]{:S(2)}) async-start(), calls=%async_computation.4 | async-start | bytes 1769472
  21.4 1.7 copy-start.12
  22.8 1.0 copy-start.11
  23.1 1.0 copy-start.10
  24.1 0.9 copy-start.9
  24.3 1.0 copy-start.8
  25.0 1.0 copy-start.7
  26.0 8.6 %copy-start.6 = (bf16[1,16,32,256]{3,2,1,0:T(8,128)(2,1)S(1)}, bf16[1,16,32,256]{3,2,1,0:T(8,128)(2,1)}, u32[]{:S(2)}) copy-start(bf16[1,16,32,256]{3,2,1,0:T(8,128)(2,1)} %get-tuple-element.22) | copy-start | bytes 786436
  33.4 2.4 %copy-start.13 = (bf16[9,256,256]{2,1,0:T(8,128)(2,1)S(1)}, bf16[9,256,256]{2,1,0:T(8,128)(2,1)}, u32[]{:S(2)}) copy-start(bf16[9,256,256]{2,1,0:T(8,128)(2,1)} %all-gather.3.cloned.1.call-done) | copy-start | bytes 3538948
  36.7 1.0 copy-start.17
  37.6 1.0 copy-start.16
  37.6 1.1 copy-start.18
  45.7 1.0 copy-start.15
  45.7 1.2 copy-start.5
  45.7 22.1 %reduce-scatter.9.cloned.1.call-start = ((), (), s32[]{:S(2)}) async-start(), calls=%async_computation.5 | async-start | bytes 1769472
  46.9 2.9 %copy-start.2 = (bf16[1,16,32,256]{3,2,1,0:T(8,128)(2,1)}, bf16[1,16,32,256]{3,2,1,0:T(8,128)(2,1)S(1)}, u32[]{:S(2)}) copy-start(bf16[1,16,32,256]{3,2,1,0:T(8,128)(2,1)S(1)} %multiply_convert_fusion.3) | copy-start | bytes 786436
  47.8 1.0 copy-start.19
  52.3 1.6 copy-start.3
  54.2 1.3 copy-start
  56.0 1.0 copy-start.20
  (1 other events, 0.8 us)
Sparse Core Ops, SparseCore 0:
  9.5 11.8 all-gather.4
  23.0 10.3 all-gather.2
  45.9 9.8 reduce-scatter.6
  57.9 9.8 reduce-scatter.8
where the time goes:
time: 178 us
  blocking collectives  98.7 us (55%)
  waiting for transfers between devices  24.6 us (14%)
  local copies, waits for them, and re-layouts  21.6 us (12%)
  matrix products  14.9 us (8%)
  between operations  14.2 us (8%)
  other arithmetic  3.46 us (2%)
    psum x1, blocking collectives, body(): first_sum, second_sum = lax.psum((first_half, second_half), 'dp')  98.7 us
    unnamed x50, local copies, waits for them, and re-layouts  17.4 us
    all_gather x1, waiting for transfers between devices, body(): lax.all_gather(conv_second, 'shard', axis=2, tiled=True)  10.2 us
    dot_general x27, matrix products, conv_taps(): jnp.dot(window, kernel[tap], preferred_element_type=jnp.float32)  9.95 us
    unnamed x6, waiting for transfers between devices  8.06 us
    all_gather x1, waiting for transfers between devices, body(): lax.all_gather(conv_first, 'shard', axis=2, tiled=True)  6.31 us
    dot_general x18, matrix products, weight_terms(): lax.dot_general(window, grad_flat, (((0,), (0,)), ((), ())), preferred_el...  4.97 us
  transfers between devices with their start and end apart: 4, of which 3 were waited for; matrix products, arithmetic and copies ran while one was open for 10% of the time, Pallas kernels for 0%

commit v1 on v0

v1 whole, which is shorter than its diff:
```python
import functools

import jax
import jax.numpy as jnp
from jax import lax
from jax.experimental import pallas as pl
from jax.experimental.pallas import tpu as pltpu
from jax.sharding import PartitionSpec as P

MESH = pl.DeviceIdType.MESH
F32 = jnp.float32
BF16 = jnp.bfloat16
SUB = 1

PAIR, XRS, ZIN, ZMID, GZ, GX = range(6)


def remote(src, dst, ssem, rsem, dev):
    return pltpu.make_async_remote_copy(
        src_ref=src, dst_ref=dst, send_sem=ssem, recv_sem=rsem, device_id=dev, device_id_type=MESH
    )


def spread(dst, value, cols):
    cells, chans = value.shape
    j = lax.broadcasted_iota(jnp.int32, value.shape, 0) % cols
    zeros = jnp.zeros((cols, 3 * chans), BF16)
    dst[0:cols, :] = zeros
    dst[cells + cols : cells + 2 * cols, :] = zeros
    after = jnp.where(j == 0, 0.0, pltpu.roll(value, 1, 0))
    dst[cols : cells + cols, 0:chans] = after.astype(BF16)
    dst[cols : cells + cols, chans : 2 * chans] = value.astype(BF16)
    before = jnp.where(j == cols - 1, 0.0, pltpu.roll(value, cells - 1, 0))
    dst[cols : cells + cols, 2 * chans : 3 * chans] = before.astype(BF16)


def kernel(
    dims, x_hbm, g_hbm, w1_hbm, w2_hbm, out_hbm, g2_hbm, g1_hbm,
    xv, gv, wb1, wb2, sx, sh, sg, pre, gt, dt, ov,
    own, psend, precv, xsend, xrecv, zs, zin, zmid, gath,
    lsem, wsend, wrecv, ssem, rsem, osem,
):
    n, cols, scale = dims
    cells, chans = xv.shape
    half = chans // 2
    quarter = half // 2
    n_chunks, _, width = own.shape
    sub = 3 * chans // width
    line = n // 2

    dp = lax.axis_index("dp")
    me = lax.axis_index("shard")
    other = 1 - me
    xi = dp % 2
    z = dp // 2
    low = z < line // 2
    inward = jnp.where(low, z + 1, z - 1)
    outward = jnp.where(low, z - 1, z + 1)
    has_outer = jnp.logical_and(z > 0, z < line - 1)
    is_mid = jnp.logical_or(z == line // 2 - 1, z == line // 2)
    not_mid = jnp.logical_not(is_mid)
    to_pair = {"shard": other}
    to_x = {"dp": z * 2 + 1 - xi}
    to_in = {"dp": inward * 2 + xi}
    to_out = {"dp": outward * 2 + xi}

    locals_ = [
        pltpu.make_async_copy(x_hbm, xv, lsem.at[0]),
        pltpu.make_async_copy(w1_hbm, wb1.at[me], lsem.at[1]),
        pltpu.make_async_copy(g_hbm, gv, lsem.at[2]),
        pltpu.make_async_copy(w2_hbm, wb2.at[me], lsem.at[3]),
    ]
    for copy in locals_:
        copy.start()

    barrier = pltpu.get_barrier_semaphore()
    for dev in (to_pair, to_x, to_in):
        pl.semaphore_signal(barrier, inc=1, device_id=dev, device_id_type=MESH)

    @pl.when(has_outer)
    def _():
        pl.semaphore_signal(barrier, inc=1, device_id=to_out, device_id_type=MESH)

    pl.semaphore_wait(barrier, 3 + has_outer.astype(jnp.int32))

    wcopies = [
        remote(w1_hbm, wb1.at[me], wsend.at[0], wrecv.at[0], to_pair),
        remote(w2_hbm, wb2.at[me], wsend.at[1], wrecv.at[1], to_pair),
    ]
    for copy in wcopies:
        copy.start()

    my_rows = pl.ds(pl.multiple_of(xi * quarter, quarter), quarter)
    their_rows = pl.ds(pl.multiple_of((1 - xi) * quarter, quarter), quarter)

    def c_pair(q):
        return remote(psend.at[q], precv.at[q], ssem.at[PAIR, q], rsem.at[PAIR, q], to_pair)

    def c_xrs(q):
        return remote(xsend.at[q], xrecv.at[q], ssem.at[XRS, q], rsem.at[XRS, q], to_x)

    def c_zin(q):
        return remote(zs.at[q], zin.at[q], ssem.at[ZIN, q], rsem.at[ZIN, q], to_in)

    def c_zmid(q):
        return remote(zs.at[q], zmid.at[q], ssem.at[ZMID, q], rsem.at[ZMID, q], to_in)

    def c_gz(q):
        return remote(gath.at[q, my_rows], gath.at[q, my_rows], ssem.at[GZ, q], rsem.at[GZ, q], to_out)

    def c_gx(q):
        return remote(gath.at[q, my_rows], gath.at[q, my_rows], ssem.at[GX, q], rsem.at[GX, q], to_x)

    def c_out(q):
        per = n_chunks // 2
        dst = g2_hbm.at[q] if q < per else g1_hbm.at[q - per]
        return pltpu.make_async_copy(gath.at[q], dst, osem.at[q])

    def s1(q):
        c_pair(q).wait_recv()
        there = own[q, their_rows, :] + precv[q, their_rows, :].astype(F32)
        xsend[q] = there.astype(BF16)
        c_xrs(q).start()

    def s2(q):
        c_xrs(q).wait_recv()
        mine = own[q, my_rows, :] + precv[q, my_rows, :].astype(F32) + xrecv[q].astype(F32)

        @pl.when(has_outer)
        def _():
            own[q, my_rows, :] = mine

        @pl.when(jnp.logical_not(has_outer))
        def _():
            zs[q] = mine.astype(BF16)

    def s2b(q):
        @pl.when(jnp.logical_and(jnp.logical_not(has_outer), not_mid))
        def _():
            c_zin(q).start()

        @pl.when(jnp.logical_and(jnp.logical_not(has_outer), is_mid))
        def _():
            c_zmid(q).start()

    def s3(q):
        @pl.when(has_outer)
        def _():
            c_zin(q).wait_recv()
            zs[q] = (own[q, my_rows, :] + zin[q].astype(F32)).astype(BF16)

            @pl.when(is_mid)
            def _():
                c_zmid(q).start()

            @pl.when(not_mid)
            def _():
                c_zin(q).start()

    def s4(q):
        @pl.when(is_mid)
        def _():
            c_zmid(q).wait_recv()
            gath[q, my_rows, :] = ((zs[q].astype(F32) + zmid[q].astype(F32)) * scale).astype(BF16)
            c_gx(q).start()

            @pl.when(has_outer)
            def _():
                c_gz(q).start()

    def s5(q):
        @pl.when(not_mid)
        def _():
            c_gz(q).wait_recv()
            c_gx(q).start()

            @pl.when(has_outer)
            def _():
                c_gz(q).start()

    def s6(q):
        c_gx(q).wait_recv()
        c_out(q).start()

    stages = [s1, lambda q: (s2(q), s2b(q)), s3, s4, s5, s6]
    offsets = [0, 1, 2, 3, 4, 5]

    def tick(t):
        for stage, offset in reversed(list(zip(stages, offsets))):
            q = t - offset
            if 0 <= q < n_chunks:
                stage(q)

    def conv(src, kernel_halves, m0, m):
        left = jnp.concatenate([src[m0 + a * cols : m0 + a * cols + m, :] for a in range(3)], axis=1)
        right = jnp.concatenate([kernel_halves[0], kernel_halves[1]], axis=1)
        return jnp.dot(left, right, preferred_element_type=F32)

    def conv_back(src, kernel_halves, m0, m):
        left, right = [], []
        for tap in range(9):
            a, b = tap // 3, tap % 3
            rows = slice(m0 + (2 - a) * cols, m0 + (2 - a) * cols + m)
            left.append(src[rows, (2 - b) * chans : (3 - b) * chans])
            right.append(kernel_halves[0, tap * chans : (tap + 1) * chans, :])
            right.append(kernel_halves[1, tap * chans : (tap + 1) * chans, :])
        return lax.dot_general(
            jnp.concatenate(left, axis=1),
            jnp.concatenate(right, axis=1),
            (((1,), (1,)), ((), ())),
            preferred_element_type=F32,
        )

    def terms(grad_t, src, which, a):
        field = src[a * cols : a * cols + cells, :]
        there = jnp.dot(
            grad_t[pl.ds(pl.multiple_of(other * half, half), half), :], field, preferred_element_type=F32
        ).astype(BF16)
        for s in range(sub):
            q = (which * 3 + a) * sub + s
            psend[q] = there[:, s * width : (s + 1) * width]
            c_pair(q).start()
        here = jnp.dot(
            grad_t[pl.ds(pl.multiple_of(me * half, half), half), :], field, preferred_element_type=F32
        )
        for s in range(sub):
            q = (which * 3 + a) * sub + s
            own[q] = here[:, s * width : (s + 1) * width]

    tile = min(256, cells)
    locals_[0].wait()
    spread(sx, xv[...].astype(F32), cols)
    locals_[2].wait()
    gt[...] = gv[...].astype(F32).T.astype(BF16)
    spread(sg, gv[...].astype(F32), cols)
    locals_[1].wait()
    wcopies[0].wait_recv()
    for m0 in range(0, cells, tile):
        pre[m0 : m0 + tile, :] = conv(sx, wb1, m0, tile)
    v = pre[...]
    hidden = (v / (1.0 + jnp.exp(-v))).astype(BF16)
    spread(sh, hidden.astype(F32), cols)
    for a in range(3):
        terms(gt, sh, 0, a)
    locals_[3].wait()
    wcopies[1].wait_recv()
    s1(0)
    for m0 in range(0, cells, tile):
        back = conv_back(sg, wb2, m0, tile)
        v = pre[m0 : m0 + tile, :]
        sigma = 1.0 / (1.0 + jnp.exp(-v))
        dpre = back * sigma * (1.0 + v * (1.0 - sigma))
        dt[:, m0 : m0 + tile] = dpre.T.astype(BF16)
    per = n_chunks // 2
    done = 1
    for t in range(1, sub):
        tick(t)
        done = t + 1
    for a in range(3):
        terms(dt, sx, 1, a)
        for _ in range(sub):
            tick(done)
            done += 1
    m_out = min(128, cells)
    for m0 in range(0, cells, m_out):
        total = conv(sh, wb2, m0, m_out) + xv[m0 : m0 + m_out, :].astype(F32)
        ov[m0 : m0 + m_out, :] = total.astype(BF16)
        if done < n_chunks + offsets[-1]:
            tick(done)
            done += 1
    out_copy = pltpu.make_async_copy(ov, out_hbm, lsem.at[4])
    out_copy.start()
    while done < n_chunks + offsets[-1]:
        tick(done)
        done += 1

    for copy in wcopies:
        copy.wait_send()
    for q in range(n_chunks):
        c_pair(q).wait_send()
        c_xrs(q).wait_send()
        c_gx(q).wait_send()

        @pl.when(is_mid)
        def _():
            c_zmid(q).wait_send()

        @pl.when(not_mid)
        def _():
            c_zin(q).wait_send()

        @pl.when(has_outer)
        def _():
            c_gz(q).wait_send()

        c_out(q).wait()
    out_copy.wait()


def body(mesh, inputs, cotangent, conv_first, conv_second):
    _, rows, cols, chans = inputs.shape
    cells = rows * cols
    half = chans // 2
    n = mesh.shape["dp"]
    scale = 1.0 / (inputs.shape[0] * n * mesh.shape["shard"])
    width = 3 * chans // SUB
    n_chunks = 6 * SUB
    per = n_chunks // 2
    hbm = pl.BlockSpec(memory_space=pl.ANY)
    vm = pltpu.VMEM
    outputs, second, first = pl.pallas_call(
        functools.partial(kernel, (n, cols, scale)),
        out_shape=(
            jax.ShapeDtypeStruct((cells, chans), BF16),
            jax.ShapeDtypeStruct((per, half, width), BF16),
            jax.ShapeDtypeStruct((per, half, width), BF16),
        ),
        in_specs=[hbm] * 4,
        out_specs=(hbm, hbm, hbm),
        scratch_shapes=[
            vm((cells, chans), BF16),
            vm((cells, chans), BF16),
            vm((2, 9 * chans, half), BF16),
            vm((2, 9 * chans, half), BF16),
            vm((cells + 2 * cols, 3 * chans), BF16),
            vm((cells + 2 * cols, 3 * chans), BF16),
            vm((cells + 2 * cols, 3 * chans), BF16),
            vm((cells, chans), F32),
            vm((chans, cells), BF16),
            vm((chans, cells), BF16),
            vm((cells, chans), BF16),
            vm((n_chunks, half, width), F32),
            vm((n_chunks, half, width), BF16),
            vm((n_chunks, half, width), BF16),
            vm((n_chunks, half // 2, width), BF16),
            vm((n_chunks, half // 2, width), BF16),
            vm((n_chunks, half // 2, width), BF16),
            vm((n_chunks, half // 2, width), BF16),
            vm((n_chunks, half // 2, width), BF16),
            vm((n_chunks, half, width), BF16),
            pltpu.SemaphoreType.DMA((5,)),
            pltpu.SemaphoreType.DMA((2,)),
            pltpu.SemaphoreType.DMA((2,)),
            pltpu.SemaphoreType.DMA((6, n_chunks)),
            pltpu.SemaphoreType.DMA((6, n_chunks)),
            pltpu.SemaphoreType.DMA((n_chunks,)),
        ],
        compiler_params=pltpu.CompilerParams(
            collective_id=0, has_side_effects=True, vmem_limit_bytes=40 * 1024 * 1024
        ),
    )(
        inputs.reshape(cells, chans),
        cotangent.reshape(cells, chans),
        conv_first.reshape(9 * chans, half),
        conv_second.reshape(9 * chans, half),
    )

    def laid(grad):
        taps = grad.reshape(3, SUB, half, 3 // SUB, chans)
        return jnp.transpose(taps, (0, 1, 3, 4, 2)).reshape(9, chans, half)

    return outputs.reshape(inputs.shape), laid(first), laid(second)


def solution(mesh):
    placed = (
        P(("group", "dp", "shard"), None, None, None),
        P(("group", "dp", "shard"), None, None, None),
        P("group", None, "shard"),
        P("group", None, "shard"),
    )
    return jax.shard_map(
        functools.partial(body, mesh),
        mesh=mesh,
        in_specs=placed,
        out_specs=(
            P(("group", "dp", "shard"), None, None, None),
            P("group", None, "shard"),
            P("group", None, "shard"),
        ),
        check_vma=False,
    )
```

time: 178 us -> 58.7 us (0.33)
  blocking collectives: 98.7 us -> 0 us
  Pallas kernels: 0 us -> 51 us
  waiting for transfers between devices: 24.6 us -> 0 us
  matrix products: 14.9 us -> 0 us
  local copies, waits for them, and re-layouts: 21.6 us -> 6.83 us
  between operations: 14.2 us -> 0.65 us
  other arithmetic: 3.46 us -> 0 us
    psum x1 -> x0, blocking collectives: 98.7 us -> none  [body(): first_sum, second_sum = lax.psum((first_half, second_half), 'dp')]
    pallas_call x0 -> x1, Pallas kernels: none -> 51 us  [body(): pl.pallas_call(functools.partial(kernel, (n, cols, scale)), out_shape=(ja...]
    all_gather x2 -> x0, waiting for transfers between devices: 16.5 us -> none  [the longest x1 10.2 us: body(): lax.all_gather(conv_second, 'shard', axis=2, tiled=True)]
    dot_general x45 -> x0, matrix products: 14.9 us -> none  [the longest x27 9.95 us: conv_taps(): jnp.dot(window, kernel[tap], preferred_element_type=jnp.float32)]
    unnamed x50 -> x9, local copies, waits for them, and re-layouts: 17.4 us -> 4.72 us
    unnamed x6 -> x0, waiting for transfers between devices: 8.06 us -> none
    convert_element_type x3 -> x0, other arithmetic: 3.46 us -> none  [the longest x1 2.52 us: body(): grad_second = (second_sum * scale).astype(jnp.bfloat16)]
    slice x3 -> x0, local copies, waits for them, and re-layouts: 2.81 us -> none  [conv_taps(): padded[:, above:above + rows, left:left + cols, :].reshape(-1, chans)]
  transfers between devices with their start and end apart: 4 -> 0, of which waited for: 3 -> 0; matrix products, arithmetic and copies ran while one was open for 10% -> 0% of each run, Pallas kernels for 0% -> 0%
where the time goes in v1:
time: 58.7 us; the launch traced here: 58.4 us
  Pallas kernels  51 us (87%)
  local copies, waits for them, and re-layouts  6.83 us (12%)
  between operations  0.65 us (1%)
    pallas_call x1, Pallas kernels, body(): pl.pallas_call(functools.partial(kernel, (n, cols, scale)), out_shape=(ja...  51 us
    unnamed x9, local copies, waits for them, and re-layouts  4.72 us
    pallas_call x2, local copies, waits for them, and re-layouts, body(): pl.pallas_call(functools.partial(kernel, (n, cols, scale)), out_shape=(ja...  2.11 us

profile of v1, /device:TPU:0, one launch (start us, length us, event | category | flops | bytes accessed | tf_op | source)
XLA Modules:
  0.0 58.4 jit_solution(7215428082536546510)
XLA Ops:
  0.6 0.0 copy-start
  0.6 1.1 %copy-done = bf16[9,256,128]{2,1,0:T(8,128)(2,1)S(1)} copy-done((bf16[9,256,128]{2,1,0:T(8,128)(2,1)S(1)}, bf16[9,256,128]{2,1,0:T(8,128)(2,1)}, u32[]{:S(2)}) %copy-start) | copy-done | bytes 589848
  1.7 0.0 copy-start.1
  1.7 1.1 %copy-done.1 = bf16[9,256,128]{2,1,0:T(8,128)(2,1)S(1)} copy-done((bf16[9,256,128]{2,1,0:T(8,128)(2,1)S(1)}, bf16[9,256,128]{2,1,0:T(8,128)(2,1)}, u32[]{:S(2)}) %copy-start.1) | copy-done | bytes 589848
  2.8 0.0 copy-start.2
  2.8 0.9 %copy-done.2 = bf16[1,16,32,256]{3,2,1,0:T(8,128)(2,1)S(1)} copy-done((bf16[1,16,32,256]{3,2,1,0:T(8,128)(2,1)S(1)}, bf16[1,16,32,256]{3,2,1,0:T(8,128)(2,1)}, u32[]{:S(2)}) %copy-start.2) | copy-done | bytes 262168
  3.7 0.0 copy-start.3
  3.7 0.9 %copy-done.3 = bf16[1,16,32,256]{3,2,1,0:T(8,128)(2,1)S(1)} copy-done((bf16[1,16,32,256]{3,2,1,0:T(8,128)(2,1)S(1)}, bf16[1,16,32,256]{3,2,1,0:T(8,128)(2,1)}, u32[]{:S(2)}) %copy-start.3) | copy-done | bytes 262168
  4.7 51.0 %shard_map.67 = (bf16[512,256]{1,0:T(8,128)(2,1)S(1)}, bf16[3,128,768]{2,1,0:T(8,128)(2,1)S(1)}, bf16[3,128,768]{2,1,0:T(8,128)(2,1)S(1)}) custom-call(bf16[512,256]{1,0:T(8,128)(2,1)S(1)} %bitcast.18, bf16[512,256]{1,0:T(8,128)(2,1)S(1)} %bitcast.19, bf16[2304,128]{1,0:T(8,128)(2,1)S(1)} %bitcast.15, bf16[2304,128]{1,0:T(8,128)(2,1)S(1)} %bitcast.16), custom_call_target="tpu_custom_call" | custom-call | tf_op jit(solution)/shard_map/pallas_call | solution.py:311
  55.6 1.1 %copy.9 = bf16[3,128,768]{1,2,0:T(8,128)(2,1)} copy(bf16[3,128,768]{2,1,0:T(8,128)(2,1)S(1)} %get-tuple-element.7) | data formatting | bytes 1179648 | tf_op jit(solution)/shard_map/pallas_call | solution.py:311
  56.7 1.1 %copy.10 = bf16[3,128,768]{1,2,0:T(8,128)(2,1)} copy(bf16[3,128,768]{2,1,0:T(8,128)(2,1)S(1)} %get-tuple-element.8) | data formatting | bytes 1179648 | tf_op jit(solution)/shard_map/pallas_call | solution.py:311
  57.7 0.7 %copy.12 = bf16[1,16,32,256]{3,2,1,0:T(8,128)(2,1)} copy(bf16[1,16,32,256]{3,2,1,0:T(8,128)(2,1)S(1)} %bitcast.17) | data formatting | bytes 524288
Async XLA Ops:
  0.6 1.1 %copy-start = (bf16[9,256,128]{2,1,0:T(8,128)(2,1)S(1)}, bf16[9,256,128]{2,1,0:T(8,128)(2,1)}, u32[]{:S(2)}) copy-start(bf16[9,256,128]{2,1,0:T(8,128)(2,1)} %param.6) | copy-start | bytes 1769476
  1.7 1.1 %copy-start.1 = (bf16[9,256,128]{2,1,0:T(8,128)(2,1)S(1)}, bf16[9,256,128]{2,1,0:T(8,128)(2,1)}, u32[]{:S(2)}) copy-start(bf16[9,256,128]{2,1,0:T(8,128)(2,1)} %param.7) | copy-start | bytes 1769476
  2.8 0.9 %copy-start.2 = (bf16[1,16,32,256]{3,2,1,0:T(8,128)(2,1)S(1)}, bf16[1,16,32,256]{3,2,1,0:T(8,128)(2,1)}, u32[]{:S(2)}) copy-start(bf16[1,16,32,256]{3,2,1,0:T(8,128)(2,1)} %param.4) | copy-start | bytes 786436
  3.7 0.9 %copy-start.3 = (bf16[1,16,32,256]{3,2,1,0:T(8,128)(2,1)S(1)}, bf16[1,16,32,256]{3,2,1,0:T(8,128)(2,1)}, u32[]{:S(2)}) copy-start(bf16[1,16,32,256]{3,2,1,0:T(8,128)(2,1)} %param.5) | copy-start | bytes 786436

commit v2 on v1

--- a/solution.py
+++ b/solution.py
@@ -10,7 +10,9 @@
 MESH = pl.DeviceIdType.MESH
 F32 = jnp.float32
 BF16 = jnp.bfloat16
-SUB = 1
+SUB = 3
+ROUTES = "A"
+STEP = 5
 
 PAIR, XRS, ZIN, ZMID, GZ, GX = range(6)
 
@@ -37,7 +39,7 @@
 def kernel(
     dims, x_hbm, g_hbm, w1_hbm, w2_hbm, out_hbm, g2_hbm, g1_hbm,
     xv, gv, wb1, wb2, sx, sh, sg, pre, gt, dt, ov,
-    own, psend, precv, xsend, xrecv, zs, zin, zmid, gath,
+    own, psend, precv, xsend, xrecv, zs, zin, zmid, gath, fs, fin, ob,
     lsem, wsend, wrecv, ssem, rsem, osem,
 ):
     n, cols, scale = dims
@@ -113,8 +115,15 @@
 
     def c_out(q):
         per = n_chunks // 2
-        dst = g2_hbm.at[q] if q < per else g1_hbm.at[q - per]
-        return pltpu.make_async_copy(gath.at[q], dst, osem.at[q])
+        taps = width // chans
+        dst = g2_hbm if q < per else g1_hbm
+        at = q % per * taps
+        return pltpu.make_async_copy(ob.at[q], dst.at[at : at + taps], osem.at[q])
+
+    def finish(q):
+        for k in range(width // chans):
+            ob[q, k] = gath[q, :, k * chans : (k + 1) * chans].astype(F32).T.astype(BF16)
+        c_out(q).start()
 
     def s1(q):
         c_pair(q).wait_recv()
@@ -180,16 +189,97 @@
 
     def s6(q):
         c_gx(q).wait_recv()
-        c_out(q).start()
-
-    stages = [s1, lambda q: (s2(q), s2b(q)), s3, s4, s5, s6]
-    offsets = [0, 1, 2, 3, 4, 5]
+        finish(q)
+
+    low_i = low.astype(jnp.int32)
+    z_rows = pl.ds(pl.multiple_of((1 - low_i) * quarter, quarter), quarter)
+    peer_rows = pl.ds(pl.multiple_of(low_i * quarter, quarter), quarter)
+
+    def c_fin(q):
+        return remote(fs.at[q], fin.at[q], ssem.at[ZIN, q], rsem.at[ZIN, q], to_in)
+
+    def c_frs(q):
+        return remote(fs.at[q, peer_rows], zmid.at[q], ssem.at[ZMID, q], rsem.at[ZMID, q], to_in)
+
+    def c_fag(q):
+        return remote(gath.at[q, z_rows], gath.at[q, z_rows], ssem.at[GX, q], rsem.at[GX, q], to_in)
+
+    def c_fout(q):
+        return remote(gath.at[q], gath.at[q], ssem.at[GZ, q], rsem.at[GZ, q], to_out)
+
+    def f1(q):
+        c_pair(q).wait_recv()
+
+        @pl.when(jnp.logical_not(has_outer))
+        def _():
+            fs[q] = (own[q] + precv[q].astype(F32)).astype(BF16)
+
+            @pl.when(is_mid)
+            def _():
+                c_frs(q).start()
+
+            @pl.when(not_mid)
+            def _():
+                c_fin(q).start()
+
+    def f2(q):
+        @pl.when(has_outer)
+        def _():
+            c_fin(q).wait_recv()
+            fs[q] = (own[q] + precv[q].astype(F32) + fin[q].astype(F32)).astype(BF16)
+
+            @pl.when(is_mid)
+            def _():
+                c_frs(q).start()
+
+            @pl.when(not_mid)
+            def _():
+                c_fin(q).start()
+
+    def f3(q):
+        @pl.when(is_mid)
+        def _():
+            c_frs(q).wait_recv()
+            xsend[q] = (fs[q, z_rows, :].astype(F32) + zmid[q].astype(F32)).astype(BF16)
+            c_xrs(q).start()
+
+    def f4(q):
+        @pl.when(is_mid)
+        def _():
+            c_xrs(q).wait_recv()
+            gath[q, z_rows, :] = ((xsend[q].astype(F32) + xrecv[q].astype(F32)) * scale).astype(BF16)
+            c_fag(q).start()
+
+    def f5(q):
+        @pl.when(is_mid)
+        def _():
+            c_fag(q).wait_recv()
+
+            @pl.when(has_outer)
+            def _():
+                c_fout(q).start()
+
+    def f6(q):
+        @pl.when(not_mid)
+        def _():
+            c_fout(q).wait_recv()
+
+            @pl.when(has_outer)
+            def _():
+                c_fout(q).start()
+
+        finish(q)
+
+    stages_a = [s1, lambda q: (s2(q), s2b(q)), s3, s4, s5, s6]
+    stages_f = [f1, f2, f3, f4, f5, f6]
+    offsets = [STEP * k for k in range(6)]
+    route = [ROUTES[q % len(ROUTES)] for q in range(n_chunks)]
 
     def tick(t):
-        for stage, offset in reversed(list(zip(stages, offsets))):
-            q = t - offset
+        for k in reversed(range(6)):
+            q = t - offsets[k]
             if 0 <= q < n_chunks:
-                stage(q)
+                (stages_a if route[q] == "A" else stages_f)[k](q)
 
     def conv(src, kernel_halves, m0, m):
         left = jnp.concatenate([src[m0 + a * cols : m0 + a * cols + m, :] for a in range(3)], axis=1)
@@ -244,14 +334,13 @@
         terms(gt, sh, 0, a)
     locals_[3].wait()
     wcopies[1].wait_recv()
-    s1(0)
+    tick(0)
     for m0 in range(0, cells, tile):
         back = conv_back(sg, wb2, m0, tile)
         v = pre[m0 : m0 + tile, :]
         sigma = 1.0 / (1.0 + jnp.exp(-v))
         dpre = back * sigma * (1.0 + v * (1.0 - sigma))
         dt[:, m0 : m0 + tile] = dpre.T.astype(BF16)
-    per = n_chunks // 2
     done = 1
     for t in range(1, sub):
         tick(t)
@@ -278,20 +367,37 @@
         copy.wait_send()
     for q in range(n_chunks):
         c_pair(q).wait_send()
-        c_xrs(q).wait_send()
-        c_gx(q).wait_send()
-
-        @pl.when(is_mid)
-        def _():
-            c_zmid(q).wait_send()
-
-        @pl.when(not_mid)
-        def _():
-            c_zin(q).wait_send()
-
-        @pl.when(has_outer)
-        def _():
-            c_gz(q).wait_send()
+        if route[q] == "A":
+            c_xrs(q).wait_send()
+            c_gx(q).wait_send()
+
+            @pl.when(is_mid)
+            def _():
+                c_zmid(q).wait_send()
+
+            @pl.when(not_mid)
+            def _():
+                c_zin(q).wait_send()
+
+            @pl.when(has_outer)
+            def _():
+                c_gz(q).wait_send()
+
+        else:
+
+            @pl.when(is_mid)
+            def _():
+                c_frs(q).wait_send()
+                c_xrs(q).wait_send()
+                c_fag(q).wait_send()
+
+            @pl.when(not_mid)
+            def _():
+                c_fin(q).wait_send()
+
+            @pl.when(has_outer)
+            def _():
+                c_fout(q).wait_send()
 
         c_out(q).wait()
     out_copy.wait()
@@ -305,15 +411,14 @@
     scale = 1.0 / (inputs.shape[0] * n * mesh.shape["shard"])
     width = 3 * chans // SUB
     n_chunks = 6 * SUB
-    per = n_chunks // 2
     hbm = pl.BlockSpec(memory_space=pl.ANY)
     vm = pltpu.VMEM
     outputs, second, first = pl.pallas_call(
         functools.partial(kernel, (n, cols, scale)),
         out_shape=(
             jax.ShapeDtypeStruct((cells, chans), BF16),
-            jax.ShapeDtypeStruct((per, half, width), BF16),
-            jax.ShapeDtypeStruct((per, half, width), BF16),
+            jax.ShapeDtypeStruct((9, chans, half), BF16),
+            jax.ShapeDtypeStruct((9, chans, half), BF16),
         ),
         in_specs=[hbm] * 4,
         out_specs=(hbm, hbm, hbm),
@@ -338,6 +443,9 @@
             vm((n_chunks, half // 2, width), BF16),
             vm((n_chunks, half // 2, width), BF16),
             vm((n_chunks, half, width), BF16),
+            vm((n_chunks, half, width), BF16),
+            vm((n_chunks, half, width), BF16),
+            vm((n_chunks, width // chans, chans, half), BF16),
             pltpu.SemaphoreType.DMA((5,)),
             pltpu.SemaphoreType.DMA((2,)),
             pltpu.SemaphoreType.DMA((2,)),
@@ -349,17 +457,13 @@
             collective_id=0, has_side_effects=True, vmem_limit_bytes=40 * 1024 * 1024
         ),
     )(
-        inputs.reshape(cells, chans),
-        cotangent.reshape(cells, chans),
-        conv_first.reshape(9 * chans, half),
-        conv_second.reshape(9 * chans, half),
+        pltpu.with_memory_space_constraint(inputs.reshape(cells, chans), pltpu.HBM),
+        pltpu.with_memory_space_constraint(cotangent.reshape(cells, chans), pltpu.HBM),
+        pltpu.with_memory_space_constraint(conv_first.reshape(9 * chans, half), pltpu.HBM),
+        pltpu.with_memory_space_constraint(conv_second.reshape(9 * chans, half), pltpu.HBM),
     )
 
-    def laid(grad):
-        taps = grad.reshape(3, SUB, half, 3 // SUB, chans)
-        return jnp.transpose(taps, (0, 1, 3, 4, 2)).reshape(9, chans, half)
-
-    return outputs.reshape(inputs.shape), laid(first), laid(second)
+    return outputs.reshape(inputs.shape), first, second
 
 
 def solution(mesh):

time: 58.7 us -> 43.3 us (0.74)
  Pallas kernels: 51 us -> 40.2 us
  local copies, waits for them, and re-layouts: 6.83 us -> 2.33 us
    pallas_call x1, Pallas kernels: 51 us -> 40.2 us  [body(): pl.pallas_call(functools.partial(kernel, (n, cols, scale)), out_shape=(ja...]
    unnamed x9 -> x3, local copies, waits for them, and re-layouts: 4.72 us -> 2.33 us
    pallas_call x2 -> x0, local copies, waits for them, and re-layouts: 2.11 us -> none  [body(): pl.pallas_call(functools.partial(kernel, (n, cols, scale)), out_shape=(ja...]
where the time goes in v2:
time: 43.3 us; the launch traced here: 43.2 us
  Pallas kernels  40.2 us (93%)
  local copies, waits for them, and re-layouts  2.33 us (5%)
  between operations  0.64 us (1%)
    pallas_call x1, Pallas kernels, body(): pl.pallas_call(functools.partial(kernel, (n, cols, scale)), out_shape=(ja...  40.2 us
    unnamed x3, local copies, waits for them, and re-layouts  2.33 us

profile of v2, /device:TPU:0, one launch (start us, length us, event | category | flops | bytes accessed | tf_op | source)
XLA Modules:
  0.0 43.2 jit_solution(12575810608057738044)
XLA Ops:
  0.6 40.2 %shard_map.67 = (bf16[512,256]{1,0:T(8,128)(2,1)S(1)}, bf16[9,256,128]{2,1,0:T(8,128)(2,1)S(1)}, bf16[9,256,128]{2,1,0:T(8,128)(2,1)S(1)}) custom-call(bf16[512,256]{1,0:T(8,128)(2,1)} %bitcast.8, bf16[512,256]{1,0:T(8,128)(2,1)} %bitcast.9, bf16[2304,128]{1,0:T(8,128)(2,1)} %bitcast.6, bf16[2304,128]{1,0:T(8,128)(2,1)} %bitcast.7), custom_call_target="tpu_custom_call" | custom-call | tf_op jit(solution)/shard_map/pallas_call | solution.py:416
  40.8 0.7 %copy.10 = bf16[1,16,32,256]{3,2,1,0:T(8,128)(2,1)} copy(bf16[1,16,32,256]{3,2,1,0:T(8,128)(2,1)S(1)} %bitcast.5) | data formatting | bytes 524288
  41.5 0.8 %copy.11 = bf16[9,256,128]{2,1,0:T(8,128)(2,1)} copy(bf16[9,256,128]{2,1,0:T(8,128)(2,1)S(1)} %get-tuple-element.13) | data formatting | bytes 1179648
  42.4 0.8 %copy.12 = bf16[9,256,128]{2,1,0:T(8,128)(2,1)} copy(bf16[9,256,128]{2,1,0:T(8,128)(2,1)S(1)} %get-tuple-element.14) | data formatting | bytes 1179648

commit v3 on v2

--- a/solution.py
+++ b/solution.py
@@ -12,7 +12,7 @@
 BF16 = jnp.bfloat16
 SUB = 3
 ROUTES = "A"
-STEP = 5
+STEP = 6
 
 PAIR, XRS, ZIN, ZMID, GZ, GX = range(6)
 
@@ -37,10 +37,10 @@
 
 
 def kernel(
-    dims, x_hbm, g_hbm, w1_hbm, w2_hbm, out_hbm, g2_hbm, g1_hbm,
-    xv, gv, wb1, wb2, sx, sh, sg, pre, gt, dt, ov,
-    own, psend, precv, xsend, xrecv, zs, zin, zmid, gath, fs, fin, ob,
-    lsem, wsend, wrecv, ssem, rsem, osem,
+    dims, x_hbm, g_hbm, w1_hbm, w2_hbm, out_ref, g2_ref, g1_ref,
+    xv, gv, wb1, wb2, sx, sh, sg, pre, gt, dt,
+    own, psend, precv, xsend, xrecv, zs, zin, zmid, gath, fs, fin,
+    lsem, wsend, wrecv, ssem, rsem,
 ):
     n, cols, scale = dims
     cells, chans = xv.shape
@@ -89,8 +89,7 @@
         remote(w1_hbm, wb1.at[me], wsend.at[0], wrecv.at[0], to_pair),
         remote(w2_hbm, wb2.at[me], wsend.at[1], wrecv.at[1], to_pair),
     ]
-    for copy in wcopies:
-        copy.start()
+    wcopies[0].start()
 
     my_rows = pl.ds(pl.multiple_of(xi * quarter, quarter), quarter)
     their_rows = pl.ds(pl.multiple_of((1 - xi) * quarter, quarter), quarter)
@@ -113,17 +112,12 @@
     def c_gx(q):
         return remote(gath.at[q, my_rows], gath.at[q, my_rows], ssem.at[GX, q], rsem.at[GX, q], to_x)
 
-    def c_out(q):
+    def finish(q):
         per = n_chunks // 2
         taps = width // chans
-        dst = g2_hbm if q < per else g1_hbm
-        at = q % per * taps
-        return pltpu.make_async_copy(ob.at[q], dst.at[at : at + taps], osem.at[q])
-
-    def finish(q):
-        for k in range(width // chans):
-            ob[q, k] = gath[q, :, k * chans : (k + 1) * chans].astype(F32).T.astype(BF16)
-        c_out(q).start()
+        dst = g2_ref if q < per else g1_ref
+        for k in range(taps):
+            dst[q % per * taps + k] = gath[q, :, k * chans : (k + 1) * chans].astype(F32).T.astype(BF16)
 
     def s1(q):
         c_pair(q).wait_recv()
@@ -322,9 +316,9 @@
     spread(sx, xv[...].astype(F32), cols)
     locals_[2].wait()
     gt[...] = gv[...].astype(F32).T.astype(BF16)
-    spread(sg, gv[...].astype(F32), cols)
     locals_[1].wait()
     wcopies[0].wait_recv()
+    wcopies[1].start()
     for m0 in range(0, cells, tile):
         pre[m0 : m0 + tile, :] = conv(sx, wb1, m0, tile)
     v = pre[...]
@@ -332,6 +326,7 @@
     spread(sh, hidden.astype(F32), cols)
     for a in range(3):
         terms(gt, sh, 0, a)
+    spread(sg, gv[...].astype(F32), cols)
     locals_[3].wait()
     wcopies[1].wait_recv()
     tick(0)
@@ -353,12 +348,10 @@
     m_out = min(128, cells)
     for m0 in range(0, cells, m_out):
         total = conv(sh, wb2, m0, m_out) + xv[m0 : m0 + m_out, :].astype(F32)
-        ov[m0 : m0 + m_out, :] = total.astype(BF16)
+        out_ref[m0 : m0 + m_out, :] = total.astype(BF16)
         if done < n_chunks + offsets[-1]:
             tick(done)
             done += 1
-    out_copy = pltpu.make_async_copy(ov, out_hbm, lsem.at[4])
-    out_copy.start()
     while done < n_chunks + offsets[-1]:
         tick(done)
         done += 1
@@ -398,9 +391,6 @@
             @pl.when(has_outer)
             def _():
                 c_fout(q).wait_send()
-
-        c_out(q).wait()
-    out_copy.wait()
 
 
 def body(mesh, inputs, cotangent, conv_first, conv_second):
@@ -421,7 +411,7 @@
             jax.ShapeDtypeStruct((9, chans, half), BF16),
         ),
         in_specs=[hbm] * 4,
-        out_specs=(hbm, hbm, hbm),
+        out_specs=(pl.BlockSpec(memory_space=vm),) * 3,
         scratch_shapes=[
             vm((cells, chans), BF16),
             vm((cells, chans), BF16),
@@ -433,7 +423,6 @@
             vm((cells, chans), F32),
             vm((chans, cells), BF16),
             vm((chans, cells), BF16),
-            vm((cells, chans), BF16),
             vm((n_chunks, half, width), F32),
             vm((n_chunks, half, width), BF16),
             vm((n_chunks, half, width), BF16),
@@ -445,13 +434,11 @@
             vm((n_chunks, half, width), BF16),
             vm((n_chunks, half, width), BF16),
             vm((n_chunks, half, width), BF16),
-            vm((n_chunks, width // chans, chans, half), BF16),
-            pltpu.SemaphoreType.DMA((5,)),
+            pltpu.SemaphoreType.DMA((4,)),
             pltpu.SemaphoreType.DMA((2,)),
             pltpu.SemaphoreType.DMA((2,)),
             pltpu.SemaphoreType.DMA((6, n_chunks)),
             pltpu.SemaphoreType.DMA((6, n_chunks)),
-            pltpu.SemaphoreType.DMA((n_chunks,)),
         ],
         compiler_params=pltpu.CompilerParams(
             collective_id=0, has_side_effects=True, vmem_limit_bytes=40 * 1024 * 1024

time: 43.3 us -> 42.4 us (0.979)
  Pallas kernels: 40.2 us -> 39.2 us
    pallas_call x1, Pallas kernels: 40.2 us -> 39.2 us  [body(): pl.pallas_call(functools.partial(kernel, (n, cols, scale)), out_shape=(ja...]
where the time goes in v3:
time: 42.4 us; the launch traced here: 42.2 us
  Pallas kernels  39.2 us (92%)
  local copies, waits for them, and re-layouts  2.33 us (5%)
  between operations  0.64 us (2%)
    pallas_call x1, Pallas kernels, body(): pl.pallas_call(functools.partial(kernel, (n, cols, scale)), out_shape=(ja...  39.2 us
    unnamed x3, local copies, waits for them, and re-layouts  2.33 us

profile of v3, /device:TPU:0, one launch (start us, length us, event | category | flops | bytes accessed | tf_op | source)
XLA Modules:
  0.0 42.2 jit_solution(4666816362009347856)
XLA Ops:
  0.6 39.2 %shard_map.67 = (bf16[512,256]{1,0:T(8,128)(2,1)S(1)}, bf16[9,256,128]{2,1,0:T(8,128)(2,1)S(1)}, bf16[9,256,128]{2,1,0:T(8,128)(2,1)S(1)}) custom-call(bf16[512,256]{1,0:T(8,128)(2,1)} %bitcast.8, bf16[512,256]{1,0:T(8,128)(2,1)} %bitcast.9, bf16[2304,128]{1,0:T(8,128)(2,1)} %bitcast.6, bf16[2304,128]{1,0:T(8,128)(2,1)} %bitcast.7), custom_call_target="tpu_custom_call" | custom-call | tf_op jit(solution)/shard_map/pallas_call | solution.py:406
  39.9 0.7 %copy.10 = bf16[1,16,32,256]{3,2,1,0:T(8,128)(2,1)} copy(bf16[1,16,32,256]{3,2,1,0:T(8,128)(2,1)S(1)} %bitcast.5) | data formatting | bytes 524288
  40.6 0.8 %copy.11 = bf16[9,256,128]{2,1,0:T(8,128)(2,1)} copy(bf16[9,256,128]{2,1,0:T(8,128)(2,1)S(1)} %get-tuple-element.13) | data formatting | bytes 1179648
  41.4 0.8 %copy.12 = bf16[9,256,128]{2,1,0:T(8,128)(2,1)} copy(bf16[9,256,128]{2,1,0:T(8,128)(2,1)S(1)} %get-tuple-element.14) | data formatting | bytes 1179648
